TPU v7x, 32 devices: a whole 2x2x4 slice. The times are simulated.
32 devices in a mesh: parts: 2 (over y), design: 4 (over z), dap: 4 (over x, core).
Axes of the slice: x: 2, y: 2, z: 4, core: 2. Of those that a mesh axis runs over, the one named last changes fastest.
Arguments:
- pair: bfloat16 [8, 256, 256, 128], P(('parts', 'design'), 'dap'), parts along dimension 0, may hold values from -6 to 6
- lengths: int32 [8], P(('parts', 'design')), parts along dimension 0, may hold values from 64 to 256, as said below
- attn_gain: float32 [2, 128], replicated, may hold values from 0.1 to 1.9
- attn_proj: bfloat16 [2, 128, 512], replicated, may hold values from -0.5 to 0.5
- attn_bias: bfloat16 [2, 128, 4], replicated, may hold values from -0.5 to 0.5
- attn_out: bfloat16 [2, 128, 128], replicated, may hold values from -0.5 to 0.5
- trans_gain: float32 [128], replicated, may hold values from 0.1 to 1.9
- trans_up: bfloat16 [128, 512], replicated, may hold values from -0.5 to 0.5
- trans_down: bfloat16 [512, 128], replicated, may hold values from -0.25 to 0.25
Outputs:
- updated: bfloat16 [8, 256, 256, 128], P(('parts', 'design'), 'dap'), parts along dimension 0
There are 2 independent parts, one for each index of `parts`. A program takes and returns all parts, laid end to end along the dimension named above; an argument that names none is the same for every part. Nothing has to cross between parts.
Inputs may be any that keep to these rules, and one draw needn't show every extreme that they name: `lengths`: some protein of every group has exactly 256 residues.
All inputs are finite; a program needn't handle non-finite values.
Results may differ from a plain program's by a relative error of at most 0.008.
Values may be sent and summed in bfloat16 or wider, within the bound.
A program may use at most 128 MiB of HBM per device.

v0:
```python
import math

import jax
import jax.numpy as jnp
from jax import lax
from jax.sharding import PartitionSpec as P

EPSILON = 1e-05


def layer_norm(values, gain):
    values = values.astype(jnp.float32)
    center = values - jnp.mean(values, axis=-1, keepdims=True)
    spread = jnp.mean(center * center, axis=-1, keepdims=True)
    return center * lax.rsqrt(spread + EPSILON) * gain


def attend(pair_x, normed, bias_full, live_keys, w_proj, w_out, column):
    heads = bias_full.shape[0]
    head_size = w_out.shape[0] // heads
    form_in = "lrc,cf->rfl" if column else "rlc,cf->rfl"
    projected = jnp.einsum(form_in, normed, w_proj, preferred_element_type=jnp.float32).astype(
        jnp.bfloat16
    )
    extent = projected.shape[2]
    factor = 1.0 / math.sqrt(head_size)
    bias_wide = bias_full.astype(jnp.float32)

    def one_row(single):
        blocks = single.reshape(4, heads, head_size, extent)
        logits = jnp.einsum(
            "hdj,hdk->hjk", blocks[0], blocks[1], preferred_element_type=jnp.float32
        )
        logits = logits * factor + bias_wide
        logits = jnp.where(live_keys[None, None, :], logits, -1000000000.0)
        probs = jax.nn.softmax(logits, axis=-1).astype(jnp.bfloat16)
        mixed = jnp.einsum("hjk,hdk->hdj", probs, blocks[2], preferred_element_type=jnp.float32)
        gated = (mixed * jax.nn.sigmoid(blocks[3].astype(jnp.float32))).astype(jnp.bfloat16)
        return gated.reshape(heads * head_size, extent)

    gated = lax.map(one_row, projected)
    form_out = "rfl,fc->lrc" if column else "rfl,fc->rlc"
    update = jnp.einsum(form_out, gated, w_out, preferred_element_type=jnp.float32)
    return (pair_x.astype(jnp.float32) + update).astype(jnp.bfloat16)


def transition(pair_x, gain, w_up, w_down):
    normed = layer_norm(pair_x, gain).astype(jnp.bfloat16)
    hidden = jax.nn.relu(jnp.dot(normed, w_up, preferred_element_type=jnp.float32)).astype(
        jnp.bfloat16
    )
    out_term = jnp.dot(hidden, w_down, preferred_element_type=jnp.float32)
    return (pair_x.astype(jnp.float32) + out_term).astype(jnp.bfloat16)


def local_bias(normed, w_bias):
    form = "rlc,ch->hrl"
    return jnp.einsum(form, normed, w_bias, preferred_element_type=jnp.float32).astype(jnp.bfloat16)


def on_device(
    pair, lengths, attn_gain, attn_proj, attn_bias, attn_out, trans_gain, trans_up, trans_down
):
    current = pair[0]
    length = lengths[0]
    rows, extent, width = current.shape
    groups = lax.axis_size("dap")
    block = extent // groups
    live_keys = jnp.arange(extent, dtype=jnp.int32) < length
    normed = layer_norm(current, attn_gain[0]).astype(jnp.bfloat16)
    start_full = lax.all_gather(local_bias(normed, attn_bias[0]), "dap", axis=1, tiled=True)
    first = attend(current, normed, start_full, live_keys, attn_proj[0], attn_out[0], False)
    pieces = first.reshape(rows, groups, block, width)
    normed_rows = layer_norm(first, attn_gain[1]).astype(jnp.bfloat16)
    gathered = lax.all_gather(local_bias(normed_rows, attn_bias[1]), "dap", axis=1, tiled=True)
    end_full = jnp.swapaxes(gathered, 1, 2)
    piece = lax.all_to_all(pieces, "dap", split_axis=1, concat_axis=0, tiled=True)
    count = piece.shape[2]
    columns = piece.reshape(extent, count, width)
    normed_cols = layer_norm(columns, attn_gain[1]).astype(jnp.bfloat16)
    second = attend(columns, normed_cols, end_full, live_keys, attn_proj[1], attn_out[1], True)
    third = transition(second, trans_gain, trans_up, trans_down)
    finished = third.reshape(extent, 1, count, width)
    returned = lax.all_to_all(finished, "dap", split_axis=0, concat_axis=1, tiled=True).reshape(
        rows, extent, width
    )
    row_ids = lax.axis_index("dap") * rows + jnp.arange(rows, dtype=jnp.int32)
    keep = (row_ids < length)[:, None] & live_keys[None, :]
    result = jnp.where(keep[:, :, None], returned, jnp.zeros_like(returned))
    return result[None]


def solution(mesh):
    in_specs = (
        P(("parts", "design"), "dap", None, None),
        P(("parts", "design")),
        P(),
        P(),
        P(),
        P(),
        P(),
        P(),
        P(),
    )
    out_specs = P(("parts", "design"), "dap", None, None)
    return jax.shard_map(
        on_device, mesh=mesh, in_specs=in_specs, out_specs=out_specs, check_vma=False
    )
```

profile of v0, /device:TPU:0, one launch (start us, length us, event | category | flops | bytes accessed | tf_op | source)
XLA Modules:
  0.0 727.4 jit_solution(7110128802472918835)
XLA Ops:
  0.0 3.5 convert_reduce_fusion.1
  3.5 6.0 fusion.35
  9.6 8.5 %convert_bitcast_fusion.1 = bf16[64,512,256]{1,2,0:T(8,128)(2,1)} fusion(bf16[1,64,256,128]{3,2,1,0:T(8,128)(2,1)S(1)} %copy-done.1, f32[128]{0:T(128)S(1)} %get-tuple-element.136, f32[64,256]{1,0:T(8,128)S(1)} %add_rsqrt_fusion.3, f32[64,256]{1,0:T(8,128)S(1)} %broadcast_multiply_fusion.3, bf16[2,128,512]{2,1,0:T(8,128)(2,1)S(1)} %copy-done.4), kind=kOutput, calls=%fused_computation.40 | convolution fusion | flops 2166358016 | bytes 21234176 | tf_op jit(solution)/shard_map/rlc,cf->rfl/dot_general | solution.py:22
  18.2 5.8 fusion.69
  24.0 8.6 %all_gather.6 = bf16[4,256,256]{2,0,1:T(4,128)(2,1)S(1)} all-gather(bf16[4,64,256]{2,0,1:T(4,128)(2,1)S(1)} %fusion.69), channel_id=1, replica_groups=mesh['parts'=2,'design'=4,'dap'=4] {'dap'}, dimensions={1}, use_global_device_ids=true | all-gather | bytes 655360 | tf_op jit(solution)/shard_map/all_gather | solution.py:71
  32.9 2.5 broadcast.170.clone
  35.5 238.8 %while.22 = (s32[]{:T(128)}, bf16[64,128,256]{2,1,0:T(8,128)(2,1)}, bf16[64,512,256]{1,2,0:T(8,128)(2,1)}, f32[4,256,256]{1,2,0:T(8,128)S(1)}, s32[]{:T(128)}, /*index=5*/s32[]{:T(128)}, s32[]{:T(128)}, s32[]{}, s32[]{}, s32[]{}) while((s32[]{:T(128)}, bf16[64,128,256]{2,1,0:T(8,128)(2,1)}, bf16[64,512,256]{1,2,0:T(8,128)(2,1)}, ...), condition=%wide.region_5.6_spmd.clone, body=%wide.region_2.5_spmd.clone.sunk | while | flops 35849988 | bytes 5973149 | solution.py:41
  35.5 1.0 constant_dynamic-slice_fusion.10
  39.2 1.0 constant_dynamic-slice_fusion.10
  42.9 1.0 constant_dynamic-slice_fusion.10
  46.7 1.0 constant_dynamic-slice_fusion.10
  50.4 1.0 constant_dynamic-slice_fusion.10
  54.1 1.0 constant_dynamic-slice_fusion.10
  57.9 1.0 constant_dynamic-slice_fusion.10
  61.6 1.0 constant_dynamic-slice_fusion.10
  65.3 1.0 constant_dynamic-slice_fusion.10
  69.1 1.0 constant_dynamic-slice_fusion.10
  125.0 1.0 constant_dynamic-slice_fusion.10
  195.9 1.0 constant_dynamic-slice_fusion.10
  266.8 1.0 constant_dynamic-slice_fusion.10
  274.2 6.9 convert_reduce_fusion.2
  281.2 1.9 copy-done.2
  283.1 3.3 copy.45
  286.4 5.0 all-to-all-start
  291.4 6.0 fusion.31
  297.5 6.3 fusion.66
  303.8 39.3 %all_gather.7 = bf16[4,256,256]{2,0,1:T(4,128)(2,1)S(1)} all-gather(bf16[4,64,256]{2,0,1:T(4,128)(2,1)S(1)} %fusion.66), channel_id=1, replica_groups=mesh['parts'=2,'design'=4,'dap'=4] {'dap'}, dimensions={1}, use_global_device_ids=true | all-gather | bytes 655360 | tf_op jit(solution)/shard_map/all_gather | solution.py:75
  343.4 4.4 bitcast_reduce_fusion
  347.9 6.0 multiply_reduce_fusion
  353.9 8.8 %multiply_convert_fusion = bf16[4,64,1,64,128]{4,3,1,0,2:T(8,128)(2,1)} fusion(bf16[64,4,64,128]{3,2,0,1:T(8,128)(2,1)} %all-to-all-done, f32[128]{0:T(128)S(1)} %get-tuple-element.135, f32[4,64,64]{2,1,0:T(8,128)S(1)} %add_rsqrt_fusion, f32[4,64,64]{2,1,0:T(8,128)S(1)} %broadcast_multiply_fusion), kind=kLoop, calls=%fused_computation.73 | loop fusion | flops 10485760 | bytes 8520192 | tf_op jit(solution)/shard_map/convert_element_type | solution.py:80
  362.7 15.5 %convert_bitcast_fusion = bf16[64,512,256]{1,2,0:T(8,128)(2,1)} fusion(bf16[256,64,128]{2,1,0:T(8,128)(2,1)} %bitcast.169, bf16[2,128,512]{2,1,0:T(8,128)(2,1)S(1)} %copy-done.4), kind=kOutput, calls=%fused_computation.39 | convolution fusion | flops 2155872256 | bytes 21102592 | tf_op jit(solution)/shard_map/lrc,cf->rfl/dot_general | solution.py:22
  378.2 2.5 broadcast.170
  380.7 238.8 %while.23 = (s32[]{:T(128)}, bf16[64,128,256]{2,1,0:T(8,128)(2,1)}, bf16[64,512,256]{1,2,0:T(8,128)(2,1)}, f32[4,256,256]{1,2,0:T(8,128)S(1)}, s32[]{:T(128)}, /*index=5*/s32[]{:T(128)}, s32[]{:T(128)}, s32[]{}, s32[]{}, s32[]{}) while((s32[]{:T(128)}, bf16[64,128,256]{2,1,0:T(8,128)(2,1)}, bf16[64,512,256]{1,2,0:T(8,128)(2,1)}, ...), condition=%wide.region_13.14_spmd.clone, body=%wide.region_10.13_spmd.clone.sunk | while | flops 35849988 | bytes 5973149 | solution.py:41
  395.6 1.0 constant_dynamic-slice_fusion.11
  462.8 1.0 constant_dynamic-slice_fusion.11
  533.7 1.0 constant_dynamic-slice_fusion.11
  604.5 1.0 constant_dynamic-slice_fusion.11
  619.5 6.5 bitcast_convert_fusion
  625.9 9.2 %copy.50 = f32[256,64,128]{0,2,1:T(8,128)} copy(f32[256,64,128]{2,1,0:T(8,128)} %bitcast.168) | data formatting | bytes 16777216 | tf_op jit(solution)/shard_map/convert_element_type | solution.py:44
  635.2 6.0 convert_reduce_fusion
  641.2 2.0 copy-done.3
  643.2 1.6 fusion.28
  644.9 14.8 %fusion.42 = bf16[256,1,64,128]{0,3,2,1:T(8,128)(2,1)} fusion(bf16[256,64,128]{0,2,1:T(8,128)(2,1)} %copy-done.3, f32[128]{0:T(128)S(1)} %copy-done.9, f32[256,64]{0,1:T(8,128)S(1)} %add_rsqrt_fusion.1, f32[256,64]{0,1:T(8,128)S(1)} %broadcast_multiply_fusion.1, bf16[512,128]{1,0:T(8,128)(2,1)S(1)} %copy-done, bf16[128,512]{1,0:T(8,128)(2,1)S(1)} %copy-done.7), kind=kOutput, calls=%fused_computation.75 | convolution fusion | flops 4328521728 | bytes 8782336 | tf_op jit(solution)/shard_map/dot_general | solution.py:52
  659.6 6.4 copy.53
  666.1 4.9 all-to-all-start.1
  671.7 47.5 %all-to-all-done.1 = bf16[256,1,64,128]{3,2,1,0:T(8,128)(2,1)} async-done(((bf16[256,1,64,128]{3,2,1,0:T(8,128)(2,1)}), bf16[256,1,64,128]{3,2,1,0:T(8,128)(2,1)}, u32[]{:S(2)}, u32[]{:S(2)}) %all-to-all-start.1) | async-done | bytes 4194336 | tf_op jit(solution)/shard_map/all_to_all | solution.py:84
  719.2 3.1 copy.54
  722.3 5.1 bitcast_select_fusion
  (1425 shorter events, 454.7 us)
Async XLA Ops:
  0.0 644.8 %copy-start = (bf16[512,128]{1,0:T(8,128)(2,1)S(1)}, bf16[512,128]{1,0:T(8,128)(2,1)}, u32[]{:S(2)}) copy-start(bf16[512,128]{1,0:T(8,128)(2,1)} %param.21) | copy-start | bytes 393220
  0.0 9.6 %copy-start.1 = (bf16[1,64,256,128]{3,2,1,0:T(8,128)(2,1)S(1)}, bf16[1,64,256,128]{3,2,1,0:T(8,128)(2,1)}, u32[]{:S(2)}) copy-start(bf16[1,64,256,128]{3,2,1,0:T(8,128)(2,1)} %param.13) | copy-start | bytes 12582916
  0.0 9.6 %copy-start.6 = (f32[2,128]{1,0:T(2,128)S(1)}, f32[2,128]{1,0:T(2,128)}, u32[]{:S(2)}) copy-start(f32[2,128]{1,0:T(2,128)} %param.15) | copy-start | bytes 3076
  0.0 9.6 %copy-start.4 = (bf16[2,128,512]{2,1,0:T(8,128)(2,1)S(1)}, bf16[2,128,512]{2,1,0:T(8,128)(2,1)}, u32[]{:S(2)}) copy-start(bf16[2,128,512]{2,1,0:T(8,128)(2,1)} %param.16) | copy-start | bytes 786436
  9.6 8.6 %copy-start.8 = (bf16[2,128,4]{1,2,0:T(4,128)(2,1)S(1)}, bf16[2,128,4]{1,2,0:T(4,128)(2,1)}, u32[]{:S(2)}) copy-start(bf16[2,128,4]{1,2,0:T(4,128)(2,1)} %param.17) | copy-start | bytes 6148
  35.5 238.8 %copy-start.5 = (bf16[2,128,128]{2,1,0:T(8,128)(2,1)S(1)}, bf16[2,128,128]{2,1,0:T(8,128)(2,1)}, u32[]{:S(2)}) copy-start(bf16[2,128,128]{2,1,0:T(8,128)(2,1)} %param.18) | copy-start | bytes 196612
  281.1 1.9 copy-start.2
  286.4 57.0 %all-to-all-start = ((bf16[64,4,64,128]{3,2,0,1:T(8,128)(2,1)}), bf16[64,4,64,128]{3,2,0,1:T(8,128)(2,1)}, u32[]{:S(2)}, u32[]{:S(2)}) async-start(bf16[64,4,64,128]{3,2,0,1:T(8,128)(2,1)} %copy.45), calls=%async_computation | async-start | bytes 8388608 | tf_op jit(solution)/shard_map/all_to_all | solution.py:77
  635.2 9.7 %copy-start.7 = (bf16[128,512]{1,0:T(8,128)(2,1)S(1)}, bf16[128,512]{1,0:T(8,128)(2,1)}, u32[]{:S(2)}) copy-start(bf16[128,512]{1,0:T(8,128)(2,1)} %param.20) | copy-start | bytes 393220
  635.2 9.7 %copy-start.9 = (f32[128]{0:T(128)S(1)}, f32[128]{0:T(128)}, u32[]{:S(2)}) copy-start(f32[128]{0:T(128)} %param.19) | copy-start | bytes 1540
  641.1 2.0 copy-start.3
  666.1 53.1 %all-to-all-start.1 = ((bf16[256,1,64,128]{3,2,1,0:T(8,128)(2,1)}), bf16[256,1,64,128]{3,2,1,0:T(8,128)(2,1)}, u32[]{:S(2)}, u32[]{:S(2)}) async-start(bf16[256,1,64,128]{3,2,1,0:T(8,128)(2,1)} %copy.53), calls=%async_computation.1 | async-start | bytes 8388608 | tf_op jit(solution)/shard_map/all_to_all | solution.py:84
where the time goes:
time: 736 us; the launch traced here: 727 us
  local copies, waits for them, and re-layouts  292 us (40%)
  other arithmetic  168 us (23%)
  matrix products  154 us (21%)
  blocking collectives  47.9 us (7%)
  waiting for transfers between devices  47.5 us (6%)
  starting transfers between devices  9.9 us (1%)
  loops' own time  7.41 us (1%)
    slice x128, local copies, waits for them, and re-layouts, one_row(): blocks[1]  123 us
    lt x129, other arithmetic, on_device(): live_keys = jnp.arange(extent, dtype=jnp.int32) < length  83.5 us
    dynamic_update_slice x128, local copies, waits for them, and re-layouts, attend(): gated = lax.map(one_row, projected)  82.6 us
    while x512, local copies, waits for them, and re-layouts  54.6 us
    all_to_all x1, waiting for transfers between devices, on_device(): lax.all_to_all(finished, 'dap', split_axis=0, concat_axis=1, tiled=True)  47.5 us
    dot_general x128, matrix products, one_row(): jnp.einsum('hdj,hdk->hjk', blocks[0], blocks[1], preferred_element_type=j...  45.9 us
    dot_general x128, matrix products, one_row(): jnp.einsum('hjk,hdk->hdj', probs, blocks[2], preferred_element_type=jnp.f...  44.1 us
    all_gather x1, blocking collectives, on_device(): lax.all_gather(local_bias(normed_rows, attn_bias[1]), 'dap', axis=1, tile...  39.3 us
  transfers between devices with their start and end apart: 2, of which 1 were waited for; matrix products, arithmetic and copies ran while one was open for 2% of the time, Pallas kernels for 0%

commit v1 on v0

v1 whole, which is shorter than its diff:
```python
import functools
import math

import jax
import jax.numpy as jnp
from jax import lax
from jax.experimental import pallas as pl
from jax.experimental.pallas import tpu as pltpu
from jax.sharding import PartitionSpec as P

EPSILON = 1e-05
LOG2E = math.log2(math.e)
TILE = 16
UNROLL = 2
BF16 = jnp.bfloat16
F32 = jnp.float32
MESH = pl.DeviceIdType.MESH


def layer_norm(values, gain):
    center = values - jnp.mean(values, axis=-1, keepdims=True)
    spread = jnp.mean(center * center, axis=-1, keepdims=True)
    return (center * lax.rsqrt(spread + EPSILON) * gain).astype(BF16)


def dot_nt(left, right):
    return lax.dot_general(left, right, (((1,), (1,)), ((), ())), preferred_element_type=F32)


def dot_nn(left, right):
    return jnp.dot(left, right, preferred_element_type=F32)


def kernel(
    groups,
    heads,
    pair_ref,
    len_ref,
    gain_ref,
    proj_ref,
    wbias_ref,
    wout_ref,
    tgain_ref,
    up_ref,
    down_ref,
    out_ref,
    norm_ref,
    x2_ref,
    stage1,
    stage2,
    brow,
    bsend1,
    bsend2,
    bfull1,
    bfull2,
    bias_ref,
    turn,
    bias_send,
    bias_recv,
    one_send,
    one_recv,
    two_send,
    two_recv,
    own_sem,
):
    rows, extent, width = pair_ref.shape
    head_size = width // heads
    blocks = rows // TILE
    me = lax.axis_index("dap")
    length = len_ref[0]
    first_row = pl.multiple_of(me * rows, TILE)

    def peer(offset):
        return lax.rem(me + offset, groups)

    barrier = pltpu.get_barrier_semaphore()
    for offset in range(1, groups):
        pl.semaphore_signal(barrier, inc=1, device_id={"dap": peer(offset)}, device_id_type=MESH)
    pl.semaphore_wait(barrier, groups - 1)

    lane_head = lax.broadcasted_iota(jnp.int32, (1, width), 1) // head_size
    head_masks = [(lane_head == h).astype(F32).astype(BF16) for h in range(heads)]

    def bias_rows(index, normed, which):
        values = dot_nt(wbias_ref[which], normed)
        for part in range(extent // 128):
            half = values[:8, part * 128 : (part + 1) * 128]
            brow[part, pl.ds(pl.multiple_of(index * 8, 8), 8), :] = half

    def bias_copy(offset, which):
        src = (bsend1, bsend2)[which]
        dst = (bfull1, bfull2)[which]
        return pltpu.make_async_remote_copy(
            src_ref=src,
            dst_ref=dst.at[:, pl.ds(first_row, rows), :],
            send_sem=bias_send.at[which, offset],
            recv_sem=bias_recv.at[which, offset],
            device_id={"dap": peer(offset)},
            device_id_type=MESH,
        )

    def bias_start(which):
        src = (bsend1, bsend2)[which]
        dst = (bfull1, bfull2)[which]
        for h in range(heads):
            halves = [brow[part, pl.ds(h, rows, stride=8), :] for part in range(extent // 128)]
            piece = jnp.concatenate(halves, axis=1).astype(BF16)
            src[h] = piece
            dst[h, pl.ds(first_row, rows), :] = piece
        for offset in range(1, groups):
            bias_copy(offset, which).start()

    def bias_finish(which):
        for offset in range(1, groups):
            bias_copy(offset, which).wait()
        dst = (bfull1, bfull2)[which]
        live = lax.broadcasted_iota(jnp.int32, (1, extent), 1) < length
        for h in range(heads):
            wide = dst[h].astype(F32)
            if which == 1:
                wide = wide.T
            bias_ref[h] = jnp.where(live, wide * LOG2E, -1000000000.0)

    def attend(x, normed, which):
        projected = dot_nn(normed, proj_ref[which])
        factor = LOG2E / math.sqrt(head_size)
        query = (projected[:, :width] * factor).astype(BF16)
        keyed = projected[:, width : 2 * width].astype(BF16)
        valued = projected[:, 2 * width : 3 * width].astype(BF16)
        gate = projected[:, 3 * width :]
        probs = []
        wide_values = []
        for h in range(heads):
            logits = dot_nt(query, keyed * head_masks[h]) + bias_ref[h]
            top = jnp.max(logits, axis=-1, keepdims=True)
            probs.append(jnp.exp2(logits - top).astype(BF16))
            ones = jnp.broadcast_to(head_masks[h], (extent, width))
            wide_values.append(jnp.concatenate([valued * head_masks[h], ones], axis=1))
        mixed = dot_nn(jnp.concatenate(probs, axis=1), jnp.concatenate(wide_values, axis=0))
        gated = mixed[:, :width] / (mixed[:, width:] * (1.0 + jnp.exp(-gate)))
        return x + dot_nn(gated.astype(BF16), wout_ref[which])

    def transition(x):
        hidden = jnp.maximum(dot_nn(layer_norm(x, tgain_ref[...]), up_ref[...]), 0.0)
        return x + dot_nn(hidden.astype(BF16), down_ref[...])

    def piece_copy(block, offset, phase):
        to = pl.multiple_of(peer(offset) * rows, TILE)
        src = (stage1, stage2)[phase]
        dst = (x2_ref, out_ref)[phase]
        local = src.at[pl.ds(to, rows), pl.ds(pl.multiple_of(block * TILE, TILE), TILE), :]
        place = dst.at[:, pl.ds(pl.multiple_of(first_row + block * TILE, TILE), TILE), :]
        if offset == 0:
            return pltpu.make_async_copy(local, place, own_sem.at[phase, block])
        return pltpu.make_async_remote_copy(
            src_ref=local,
            dst_ref=place,
            send_sem=(one_send, two_send)[phase].at[block, offset],
            recv_sem=(one_recv, two_recv)[phase].at[block, offset],
            device_id={"dap": peer(offset)},
            device_id_type=MESH,
        )

    def send_block(block, phase):
        stage = (stage1, stage2)[phase]
        turned = turn[...].reshape(extent, TILE, width).astype(BF16)
        stage[:, pl.ds(pl.multiple_of(block * TILE, TILE), TILE), :] = turned
        for offset in list(range(1, groups)) + [0]:
            piece_copy(block, offset, phase).start()

    def finish_blocks(phase):
        def body(block, carry):
            for offset in range(groups):
                piece_copy(block, offset, phase).wait()
            return carry

        lax.fori_loop(0, blocks, body, 0)

    def bias_body(step, carry):
        for part in range(UNROLL):
            index = step * UNROLL + part
            normed = layer_norm(pair_ref[index].astype(F32), gain_ref[0:1])
            norm_ref[index] = normed
            bias_rows(index, normed, 0)
        return carry

    lax.fori_loop(0, rows // UNROLL, bias_body, 0)
    bias_start(0)
    bias_finish(0)

    def one_block(block, carry):
        def one_body(step, inner):
            for part in range(UNROLL):
                local = step * UNROLL + part
                index = block * TILE + local
                first = attend(pair_ref[index].astype(F32), norm_ref[index], 0)
                turn[pl.ds(local, extent, stride=TILE), :] = first
                rounded = first.astype(BF16).astype(F32)
                bias_rows(index, layer_norm(rounded, gain_ref[1:2]), 1)
            return inner

        lax.fori_loop(0, TILE // UNROLL, one_body, 0)
        send_block(block, 0)
        return carry

    lax.fori_loop(0, blocks, one_block, 0)
    bias_start(1)
    finish_blocks(0)
    bias_finish(1)

    row_live = lax.broadcasted_iota(jnp.int32, (extent, width), 0) < length

    def two_block(block, carry):
        def two_body(step, inner):
            for part in range(UNROLL):
                local = step * UNROLL + part
                index = block * TILE + local
                x = x2_ref[index].astype(F32)
                second = attend(x, layer_norm(x, gain_ref[1:2]), 1)
                third = transition(second.astype(BF16).astype(F32))
                limit = jnp.where(first_row + index < length, 1.0, 0.0)
                turn[pl.ds(local, extent, stride=TILE), :] = jnp.where(row_live, third * limit, 0.0)
            return inner

        lax.fori_loop(0, TILE // UNROLL, two_body, 0)
        send_block(block, 1)
        return carry

    lax.fori_loop(0, blocks, two_block, 0)
    finish_blocks(1)


def on_device(
    pair, lengths, attn_gain, attn_proj, attn_bias, attn_out, trans_gain, trans_up, trans_down
):
    current = pair[0]
    rows, extent, width = current.shape
    heads = attn_bias.shape[2]
    groups = lax.axis_size("dap")
    blocks = rows // TILE
    wbias = jnp.pad(jnp.swapaxes(attn_bias, 1, 2), ((0, 0), (0, 16 - heads), (0, 0)))
    vmem = pl.BlockSpec(memory_space=pltpu.VMEM)
    dma = pltpu.SemaphoreType.DMA
    result = pl.pallas_call(
        functools.partial(kernel, groups, heads),
        out_shape=jax.ShapeDtypeStruct(current.shape, BF16),
        in_specs=[vmem, pl.BlockSpec(memory_space=pltpu.SMEM)] + [vmem] * 7,
        out_specs=pl.BlockSpec(memory_space=pl.ANY),
        scratch_shapes=[
            pltpu.VMEM((rows, extent, width), BF16),
            pltpu.VMEM((rows, extent, width), BF16),
            pltpu.VMEM((extent, rows, width), BF16),
            pltpu.VMEM((extent, rows, width), BF16),
            pltpu.VMEM((extent // 128, rows * 8, 128), F32),
            pltpu.VMEM((heads, rows, extent), BF16),
            pltpu.VMEM((heads, rows, extent), BF16),
            pltpu.VMEM((heads, extent, extent), BF16),
            pltpu.VMEM((heads, extent, extent), BF16),
            pltpu.VMEM((heads, extent, extent), F32),
            pltpu.VMEM((extent * TILE, width), F32),
            dma((2, groups)),
            dma((2, groups)),
            dma((blocks, groups)),
            dma((blocks, groups)),
            dma((blocks, groups)),
            dma((blocks, groups)),
            dma((2, blocks)),
        ],
        compiler_params=pltpu.CompilerParams(
            collective_id=0, has_side_effects=True, vmem_limit_bytes=56 * 1024 * 1024
        ),
        cost_estimate=pl.CostEstimate(
            flops=20 * 1000**3, bytes_accessed=16 * 1000**2, transcendentals=40 * 1000**2
        ),
    )(current, lengths, attn_gain, attn_proj, wbias, attn_out, trans_gain[None], trans_up, trans_down)
    return result[None]


def solution(mesh):
    in_specs = (
        P(("parts", "design"), "dap", None, None),
        P(("parts", "design")),
        P(),
        P(),
        P(),
        P(),
        P(),
        P(),
        P(),
    )
    out_specs = P(("parts", "design"), "dap", None, None)
    return jax.shard_map(
        on_device, mesh=mesh, in_specs=in_specs, out_specs=out_specs, check_vma=False
    )
```

time: 736 us -> 230 us (0.31); the launches traced: 727 us -> 230 us
  local copies, waits for them, and re-layouts: 292 us -> 5.99 us
  Pallas kernels: 0 us -> 224 us
  other arithmetic: 168 us -> 0 us
  matrix products: 154 us -> 0 us
  blocking collectives: 47.9 us -> 0 us
  waiting for transfers between devices: 47.5 us -> 0 us
  starting transfers between devices: 9.9 us -> 0 us
  loops' own time: 7.41 us -> 0 us
    pallas_call x0 -> x1, Pallas kernels: none -> 224 us  [on_device(): pl.pallas_call(functools.partial(kernel, groups, heads), out_shape=jax.Sh...]
    dot_general x263 -> x0, matrix products: 154 us -> none  [the longest x128 45.9 us: one_row(): jnp.einsum('hdj,hdk->hjk', blocks[0], blocks[1], preferred_element_type=j...]
    slice x128 -> x0, local copies, waits for them, and re-layouts: 123 us -> none  [one_row(): blocks[1]]
    lt x130 -> x0, other arithmetic: 83.5 us -> none  [the longest x129 83.5 us: on_device(): live_keys = jnp.arange(extent, dtype=jnp.int32) < length]
    dynamic_update_slice x128 -> x0, local copies, waits for them, and re-layouts: 82.6 us -> none  [attend(): gated = lax.map(one_row, projected)]
    while x512 -> x0, local copies, waits for them, and re-layouts: 54.6 us -> none
    all_gather x2 -> x0, blocking collectives: 47.9 us -> none  [the longest x1 39.3 us: on_device(): lax.all_gather(local_bias(normed_rows, attn_bias[1]), 'dap', axis=1, tile...]
    all_to_all x2 -> x0, waiting for transfers between devices: 47.5 us -> none  [the longest x1 47.5 us: on_device(): lax.all_to_all(finished, 'dap', split_axis=0, concat_axis=1, tiled=True)]
  transfers between devices with their start and end apart: 2 -> 0, of which waited for: 1 -> 0; matrix products, arithmetic and copies ran while one was open for 2% -> 0% of each run, Pallas kernels for 0% -> 0%
where the time goes in v1:
time: 230 us
  Pallas kernels  224 us (97%)
  local copies, waits for them, and re-layouts  5.99 us (3%)
    pallas_call x1, Pallas kernels, on_device(): pl.pallas_call(functools.partial(kernel, groups, heads), out_shape=jax.Sh...  224 us
    unnamed x1, local copies, waits for them, and re-layouts  4.7 us

profile of v1, /device:TPU:0, one launch (start us, length us, event | category | flops | bytes accessed | tf_op | source)
XLA Modules:
  0.0 230.2 jit_solution(17966568536935966762)
XLA Ops:
  0.7 1.3 pad.4.wbias_ref
  1.9 223.5 %shard_map.91 = bf16[64,256,128]{2,1,0:T(8,128)(2,1)} custom-call(bf16[64,256,128]{2,1,0:T(8,128)(2,1)} %bitcast.6, s32[1]{0:T(128)S(6)} %copy.11.len_ref, f32[2,128]{1,0:T(2,128)} %gain_ref.1, bf16[2,128,512]{2,1,0:T(8,128)(2,1)} %proj_ref.1, bf16[2,16,128]{2,1,0:T(8,128)(2,1)} %pad.4.wbias_ref, bf16[2,128,128]{2,1,0:T(8,128)(2,1)} %wout_ref.1, ...), custom_call_target="tpu_custom_call" | custom-call | flops 20000000000 | bytes 16000000 | tf_op jit(solution)/shard_map/pallas_call | solution.py:244
  225.5 4.7 %copy.12 = bf16[1,64,256,128]{3,2,1,0:T(8,128)(2,1)} copy(bf16[1,64,256,128]{3,2,1,0:T(8,128)(2,1)} %bitcast.4) | data formatting | bytes 8388608

commit v2 on v1

--- a/solution.py
+++ b/solution.py
@@ -11,7 +11,7 @@
 EPSILON = 1e-05
 LOG2E = math.log2(math.e)
 TILE = 16
-UNROLL = 2
+UNROLL = 4
 BF16 = jnp.bfloat16
 F32 = jnp.float32
 MESH = pl.DeviceIdType.MESH
@@ -127,18 +127,21 @@
         query = (projected[:, :width] * factor).astype(BF16)
         keyed = projected[:, width : 2 * width].astype(BF16)
         valued = projected[:, 2 * width : 3 * width].astype(BF16)
-        gate = projected[:, 3 * width :]
-        probs = []
-        wide_values = []
-        for h in range(heads):
-            logits = dot_nt(query, keyed * head_masks[h]) + bias_ref[h]
-            top = jnp.max(logits, axis=-1, keepdims=True)
-            probs.append(jnp.exp2(logits - top).astype(BF16))
-            ones = jnp.broadcast_to(head_masks[h], (extent, width))
-            wide_values.append(jnp.concatenate([valued * head_masks[h], ones], axis=1))
-        mixed = dot_nn(jnp.concatenate(probs, axis=1), jnp.concatenate(wide_values, axis=0))
-        gated = mixed[:, :width] / (mixed[:, width:] * (1.0 + jnp.exp(-gate)))
-        return x + dot_nn(gated.astype(BF16), wout_ref[which])
+        gate = 1.0 + jnp.exp(-projected[:, 3 * width :])
+        ones = [jnp.broadcast_to(head_masks[h], (extent, width)) for h in range(heads)]
+        gated = []
+        for start in range(0, x.shape[0], extent):
+            span = slice(start, start + extent)
+            probs = []
+            wide_values = []
+            for h in range(heads):
+                logits = dot_nt(query[span] * head_masks[h], keyed[span]) + bias_ref[h]
+                top = jnp.max(logits, axis=-1, keepdims=True)
+                probs.append(jnp.exp2(logits - top).astype(BF16))
+                wide_values.append(jnp.concatenate([valued[span] * head_masks[h], ones[h]], axis=1))
+            mixed = dot_nn(jnp.concatenate(probs, axis=1), jnp.concatenate(wide_values, axis=0))
+            gated.append((mixed[:, :width] / (mixed[:, width:] * gate[span])).astype(BF16))
+        return x + dot_nn(jnp.concatenate(gated, axis=0), wout_ref[which])
 
     def transition(x):
         hidden = jnp.maximum(dot_nn(layer_norm(x, tgain_ref[...]), up_ref[...]), 0.0)
@@ -190,13 +193,16 @@
 
     def one_block(block, carry):
         def one_body(step, inner):
+            local = step * UNROLL
+            index = block * TILE + local
+            x = pair_ref[pl.ds(index, UNROLL)].reshape(UNROLL * extent, width).astype(F32)
+            normed = norm_ref[pl.ds(index, UNROLL)].reshape(UNROLL * extent, width)
+            first = attend(x, normed, 0)
+            renormed = layer_norm(first.astype(BF16).astype(F32), gain_ref[1:2])
             for part in range(UNROLL):
-                local = step * UNROLL + part
-                index = block * TILE + local
-                first = attend(pair_ref[index].astype(F32), norm_ref[index], 0)
-                turn[pl.ds(local, extent, stride=TILE), :] = first
-                rounded = first.astype(BF16).astype(F32)
-                bias_rows(index, layer_norm(rounded, gain_ref[1:2]), 1)
+                span = slice(part * extent, (part + 1) * extent)
+                turn[pl.ds(local + part, extent, stride=TILE), :] = first[span]
+                bias_rows(index + part, renormed[span], 1)
             return inner
 
         lax.fori_loop(0, TILE // UNROLL, one_body, 0)
@@ -212,14 +218,15 @@
 
     def two_block(block, carry):
         def two_body(step, inner):
+            local = step * UNROLL
+            index = block * TILE + local
+            x = x2_ref[pl.ds(index, UNROLL)].reshape(UNROLL * extent, width).astype(F32)
+            second = attend(x, layer_norm(x, gain_ref[1:2]), 1)
+            third = transition(second.astype(BF16).astype(F32))
             for part in range(UNROLL):
-                local = step * UNROLL + part
-                index = block * TILE + local
-                x = x2_ref[index].astype(F32)
-                second = attend(x, layer_norm(x, gain_ref[1:2]), 1)
-                third = transition(second.astype(BF16).astype(F32))
-                limit = jnp.where(first_row + index < length, 1.0, 0.0)
-                turn[pl.ds(local, extent, stride=TILE), :] = jnp.where(row_live, third * limit, 0.0)
+                limit = jnp.where(first_row + index + part < length, 1.0, 0.0)
+                piece = third[part * extent : (part + 1) * extent] * limit
+                turn[pl.ds(local + part, extent, stride=TILE), :] = jnp.where(row_live, piece, 0.0)
             return inner
 
         lax.fori_loop(0, TILE // UNROLL, two_body, 0)

time: 230 us -> 151 us (0.66)
  Pallas kernels: 224 us -> 144 us
    pallas_call x1, Pallas kernels: 224 us -> 144 us  [on_device(): pl.pallas_call(functools.partial(kernel, groups, heads), out_shape=jax.Sh...]
where the time goes in v2:
time: 151 us
  Pallas kernels  144 us (95%)
  local copies, waits for them, and re-layouts  5.99 us (4%)
    pallas_call x1, Pallas kernels, on_device(): pl.pallas_call(functools.partial(kernel, groups, heads), out_shape=jax.Sh...  144 us
    unnamed x1, local copies, waits for them, and re-layouts  4.7 us

profile of v2, /device:TPU:0, one launch (start us, length us, event | category | flops | bytes accessed | tf_op | source)
XLA Modules:
  0.0 150.7 jit_solution(12617949603489999094)
XLA Ops:
  0.7 1.3 pad.4.wbias_ref
  1.9 144.1 %shard_map.91 = bf16[64,256,128]{2,1,0:T(8,128)(2,1)} custom-call(bf16[64,256,128]{2,1,0:T(8,128)(2,1)} %bitcast.6, s32[1]{0:T(128)S(6)} %copy.11.len_ref, f32[2,128]{1,0:T(2,128)} %gain_ref.1, bf16[2,128,512]{2,1,0:T(8,128)(2,1)} %proj_ref.1, bf16[2,16,128]{2,1,0:T(8,128)(2,1)} %pad.4.wbias_ref, bf16[2,128,128]{2,1,0:T(8,128)(2,1)} %wout_ref.1, ...), custom_call_target="tpu_custom_call" | custom-call | flops 20000000000 | bytes 16000000 | tf_op jit(solution)/shard_map/pallas_call | solution.py:251
  146.0 4.7 %copy.12 = bf16[1,64,256,128]{3,2,1,0:T(8,128)(2,1)} copy(bf16[1,64,256,128]{3,2,1,0:T(8,128)(2,1)} %bitcast.4) | data formatting | bytes 8388608
